TPU v7x, 32 devices: a whole 2x2x4 slice. The times are simulated.
32 devices in a mesh: row: 8 (over z, y), col: 4 (over x, core).
Axes of the slice: x: 2, y: 2, z: 4, core: 2. Of those that a mesh axis runs over, the one named last changes fastest.
Arguments:
- leaf_basis: bfloat16 [64, 2048, 128], P(('row', 'col')), may hold values from -6 to 6
- transfer_leaf: float32 [64, 128, 128], P(('row', 'col')), may hold values from -0.5 to 0.5
- transfer_mid: float32 [32, 128, 128], P(('row', 'col')), may hold values from -0.5 to 0.5
- transfer_top: float32 [8, 2, 128, 128], P('row'), may hold values from -0.5 to 0.5
- coupling_leaf: bfloat16 [64, 112, 128, 128], P(('row', 'col')), may hold values from -6 to 6
- coupling_mid: bfloat16 [32, 112, 128, 128], P(('row', 'col')), may hold values from -6 to 6
- partners_leaf: int32 [64, 112], P(('row', 'col')), may hold values from 0 to 63, as said below
- partners_mid: int32 [32, 112], P(('row', 'col')), may hold values from 0 to 31, as said below
- counts_leaf: int32 [64], P(('row', 'col')), may hold values from 1 to 112, as said below
- counts_mid: int32 [32], P(('row', 'col')), may hold values from 1 to 112, as said below
- ranks: int32 [4], replicated, may hold values from 64 to 128
Outputs:
- leaf_q: bfloat16 [64, 2048, 128], P(('row', 'col'))
- transfer_leaf_out: float32 [64, 128, 128], P(('row', 'col'))
- transfer_mid_out: float32 [32, 128, 128], P(('row', 'col'))
- transfer_top_out: float32 [8, 4, 64, 128], P('row', 'col')
- coupling_leaf_out: bfloat16 [64, 112, 128, 128], P(('row', 'col'))
- coupling_mid_out: bfloat16 [32, 112, 128, 128], P(('row', 'col'))
Inputs may be any that keep to these rules, and one draw needn't show every extreme that they name: `partners_leaf`: A slot's partner leaf lies on a device (partner // 2) at most 6 away from the row leaf's device in the joint row-col order; distance 6 occurs. `partners_mid`: A slot's partner level-1 cluster index differs from the row cluster's by at most 6; distance 6 occurs. `counts_leaf`: some leaf has all 112 slots live. `counts_mid`: some level-1 cluster has all 112 slots live.
All inputs are finite; a program needn't handle non-finite values.
Results may differ from a plain program's by a relative error of at most 0.009.
Values sent between devices are 32-bit elements; how exact they have to be, the bound alone decides.
A program may use at most 192 MiB of HBM per device.

v0:
```python
import functools

import jax
import jax.numpy as jnp
from jax import lax
from jax.experimental import pallas as pl
from jax.experimental.pallas import tpu as pltpu
from jax.sharding import PartitionSpec as P

SPAN = 6
PANEL = 8
GROUPS = 4
CHUNK = 16
HIGHEST = lax.Precision.HIGHEST
F32 = jnp.float32
BF16 = jnp.bfloat16
MESH = pl.DeviceIdType.MESH
LIMIT = 48 * 1024 * 1024


def dot(left, right, contract, precision=None):
    return lax.dot_general(
        left, right, (contract, ((), ())), precision=precision, preferred_element_type=F32
    )


def sandwich(inner, outer):
    inner_outer = dot(inner, outer, ((1,), (0,)), HIGHEST)
    return dot(outer, inner_outer, ((0,), (0,)), HIGHEST)


def gram_kernel(basis, t_leaf, t_mid, t_top, grams, sent, landed, send_sem, recv_sem):
    leaf_count, points = basis.shape[0], basis.shape[1]
    row, col = lax.axis_index("row"), lax.axis_index("col")
    pair = lax.div(col, 2)
    siblings = (
        col + 1 - 2 * lax.rem(col, 2),
        col + 2 - 4 * lax.rem(pair, 2),
    )
    barrier = pltpu.get_barrier_semaphore()
    for other in siblings:
        pl.semaphore_signal(barrier, inc=1, device_id=(row, other), device_id_type=MESH)
    gram_mid = None
    for leaf in range(leaf_count):
        gram = dot(basis[leaf], basis[leaf], ((0,), (0,))) / points
        grams[leaf] = gram
        term = sandwich(gram, t_leaf[leaf])
        gram_mid = term if gram_mid is None else gram_mid + term
    grams[leaf_count] = gram_mid
    pl.semaphore_wait(barrier, 2)
    outer = t_mid[0]
    inner = gram_mid
    for level in range(2):
        term = sandwich(inner, outer)
        sent[level] = term
        copy = pltpu.make_async_remote_copy(
            src_ref=sent.at[level],
            dst_ref=landed.at[level],
            send_sem=send_sem.at[level],
            recv_sem=recv_sem.at[level],
            device_id=(row, siblings[level]),
            device_id_type=MESH,
        )
        copy.start()
        copy.wait()
        inner = term + landed[level]
        grams[leaf_count + 1 + level] = inner
        outer = t_top[0, pair]


def three_parts(value):
    high = value.astype(BF16).astype(F32)
    rest = value - high
    middle = rest.astype(BF16).astype(F32)
    low = rest - middle
    return high, middle, low


def eliminate(work, order):
    batch = work.shape[0]
    rows_in = lax.broadcasted_iota(jnp.int32, (PANEL, 2 * order), 0)
    lanes = lax.broadcasted_iota(jnp.int32, (PANEL, 2 * order), 1)
    narrow = lax.broadcasted_iota(jnp.int32, (PANEL, order), 0)
    lanes_narrow = lax.broadcasted_iota(jnp.int32, (PANEL, order), 1)

    def panel(index, first_row):
        base = pl.multiple_of(index * PANEL, PANEL)
        for b in range(batch):
            wide = work[b, pl.ds(base, PANEL), :]
            turned = pltpu.roll(wide[:, :order], order - base, 1)
            columns = [
                jnp.broadcast_to(turned[:, r : r + 1], (PANEL, order)) for r in range(PANEL)
            ]
            for r in range(PANEL):
                scale = lax.rsqrt(columns[r][r : r + 1, :])
                coefficient = columns[r] * scale
                scale_wide = jnp.concatenate([scale, scale], axis=1)
                coefficient_wide = jnp.concatenate([coefficient, coefficient], axis=1)
                pivot_row = wide[r : r + 1, :] * scale_wide
                wide = jnp.where(
                    rows_in > r,
                    wide - coefficient_wide * pivot_row,
                    jnp.where(rows_in == r, pivot_row, wide),
                )
                for q in range(r + 1, PANEL):
                    columns[q] = jnp.where(
                        narrow > r,
                        columns[q] - coefficient * (columns[q][r : r + 1, :] * scale),
                        columns[q],
                    )
            wide = jnp.where((lanes >= order) | (lanes >= base + rows_in), wide, 0.0)
            work[b, pl.ds(base, PANEL), :] = wide
            after = jnp.where(lanes_narrow >= base + PANEL, wide[:, :order], 0.0)
            lh, lm, ll = three_parts(after)
            rh, rm, rl = three_parts(wide)
            left = jnp.concatenate([lh, lh, lm, lh, ll, lm], axis=0).astype(BF16)
            right = jnp.concatenate([rh, rm, rh, rl, rh, rm], axis=0).astype(BF16)
            change = dot(left[:, first_row:], right, ((0,), (0,)))
            work[b, first_row:, :] = work[b, first_row:, :] - change

    panels = order // PANEL
    for group in range(GROUPS):
        first = group * panels // GROUPS
        last = (group + 1) * panels // GROUPS

        def body(index, carry):
            panel(index, first * PANEL)
            return carry

        lax.fori_loop(first, last, body, 0)


def tree_kernel(ranks, grams, basis, t_leaf, t_mid, t_top, leaf_q, leaf_out, mid_out, top_out, packed, own, work):
    leaf_count = basis.shape[0]
    order = grams.shape[1]
    half = order // 2
    row_id = lax.broadcasted_iota(jnp.int32, (order, order), 0)
    col_id = lax.broadcasted_iota(jnp.int32, (order, order), 1)
    identity = jnp.where(row_id == col_id, 1.0, 0.0).astype(F32)
    for b in range(grams.shape[0]):
        work[b, :, :order] = grams[b]
        work[b, :, order:] = identity
    eliminate(work, order)
    pair = lax.div(lax.axis_index("col"), 2)
    mid, above, quad = leaf_count, leaf_count + 1, leaf_count + 2

    def factor(b, level):
        return jnp.where(row_id < ranks[level], work[b, :, :order], 0.0)

    def inverse(b, level):
        return jnp.where(row_id < ranks[level], work[b, :, order:], 0.0)

    def moved(b, level, transfer, parent, parent_level):
        left = dot(factor(b, level), transfer, ((1,), (0,)), HIGHEST)
        return dot(left, inverse(parent, parent_level), ((1,), (1,)), HIGHEST)

    for leaf in range(leaf_count):
        weights = inverse(leaf, 0).astype(BF16)
        leaf_q[leaf] = dot(basis[leaf], weights, ((1,), (1,))).astype(BF16)
        leaf_out[leaf] = moved(leaf, 0, t_leaf[leaf], mid, 1)
    mid_out[0] = moved(mid, 1, t_mid[0], above, 2)
    top_out[...] = moved(above, 2, t_top[0, pair], quad, 3)
    first, second, third = factor(0, 0), factor(1, 0), factor(mid, 1)
    own[0] = first.astype(BF16)
    own[1] = second.astype(BF16)
    own[2] = third.astype(BF16)
    packed[:order, :] = jnp.where(col_id >= row_id, first, second.T)
    packed[order : order + half, :] = jnp.where(
        (col_id >= row_id)[:half], third[:half], shifted_transpose(third, half)
    )
    second_diagonal = jnp.sum(jnp.where(row_id == col_id, second, 0.0), axis=0, keepdims=True)
    third_diagonal = jnp.sum(jnp.where(row_id == col_id, third, 0.0), axis=0, keepdims=True)
    packed[order + half : order + half + 8, :] = jnp.broadcast_to(second_diagonal, (8, order))
    packed[order + half + 8 : order + half + 16, :] = jnp.broadcast_to(third_diagonal, (8, order))


def shifted_transpose(matrix, half):
    return pltpu.roll(matrix.T[half:], half, 1)


def exchange_kernel(devices, columns, packed, own, table, landed, send_sem, recv_sem):
    order = own.shape[1]
    half = order // 2
    here = lax.axis_index("row") * columns + lax.axis_index("col")
    barrier = pltpu.get_barrier_semaphore()
    offsets = [sign * away for away in range(1, SPAN + 1) for sign in (1, -1)]

    def place(index):
        return (lax.div(index, columns), lax.rem(index, columns))

    def inside(index):
        return (index >= 0) & (index < devices)

    for offset in offsets:
        @pl.when(inside(here + offset))
        def _():
            pl.semaphore_signal(barrier, inc=1, device_id=place(here + offset), device_id_type=MESH)
    peers = jnp.minimum(here, SPAN) + jnp.minimum(devices - 1 - here, SPAN)
    pl.semaphore_wait(barrier, peers)

    def copy_to(offset):
        slot = SPAN - offset
        return pltpu.make_async_remote_copy(
            src_ref=packed,
            dst_ref=landed.at[slot],
            send_sem=send_sem.at[slot],
            recv_sem=recv_sem.at[slot],
            device_id=place(here + offset),
            device_id_type=MESH,
        )

    for offset in reversed(offsets):
        @pl.when(inside(here + offset))
        def _():
            copy_to(offset).start()
    for k in range(3):
        table[3 * SPAN + k] = own[k]
    row_id = lax.broadcasted_iota(jnp.int32, (order, order), 0)
    col_id = lax.broadcasted_iota(jnp.int32, (order, order), 1)
    for offset in offsets:
        slot = SPAN + offset

        @pl.when(inside(here + offset))
        def _():
            copy_to(-offset).wait_recv()
            both = landed[slot, :order, :]
            upper = jnp.where(col_id >= row_id, both, 0.0)
            lower = jnp.where(
                col_id == row_id,
                landed[slot, order + half : order + half + 1, :],
                jnp.where(col_id < row_id, both, 0.0),
            )
            table[3 * slot] = upper.astype(BF16)
            table[3 * slot + 1] = lower.T.astype(BF16)
            folded = landed[slot, order : order + half, :]
            rows = row_id[:half]
            lanes = col_id[:half]
            table[3 * slot + 2, :half, :] = jnp.where(lanes >= rows, folded, 0.0).astype(BF16)
            corner = jnp.where(lanes < rows, folded, 0.0)
            corner = jnp.concatenate([corner, jnp.zeros_like(corner)], axis=0).T
            corner = pltpu.roll(corner[:half], half, 1)
            corner = jnp.where(
                lanes == rows + half, landed[slot, order + half + 8 : order + half + 9, :], corner
            )
            table[3 * slot + 2, half:, :] = corner.astype(BF16)

    for offset in offsets:
        @pl.when(inside(here + offset))
        def _():
            copy_to(offset).wait_send()


def coupling_kernel(own_first, counts, rows, blocks, table, out):
    cluster, part = pl.program_id(0), pl.program_id(1)
    count = counts[cluster]
    mine = table[3 * SPAN + own_first + cluster]
    start = part * CHUNK
    step = 4

    for sub in range(0, CHUNK, step):
        slots = range(sub, sub + step)

        @pl.when(start + sub < count)
        def _():
            lefts = [
                dot(mine, jnp.concatenate([blocks[0, s], blocks[0, s + 1]], axis=1), ((1,), (0,)))
                .astype(BF16)
                for s in slots[::2]
            ]
            order = mine.shape[0]
            for s in slots:
                left = lefts[(s - sub) // 2][:, (s - sub) % 2 * order : ((s - sub) % 2 + 1) * order]
                result = dot(left, table[rows[cluster, start + s]], ((1,), (1,)))
                out[0, s] = jnp.where(start + s < count, result, 0.0).astype(BF16)

        @pl.when(start + sub >= count)
        def _():
            out[0, sub : sub + step] = jnp.zeros((step,) + out.shape[2:], BF16)


def transform(blocks, table, rows, counts, own_first):
    clusters, slots, order, _ = blocks.shape
    parts = slots // CHUNK

    def fetched(c, p, counts, rows):
        return (c, jnp.minimum(p, lax.div(counts[c] - 1, CHUNK)), 0, 0)

    return pl.pallas_call(
        functools.partial(coupling_kernel, own_first),
        grid_spec=pltpu.PrefetchScalarGridSpec(
            num_scalar_prefetch=2,
            grid=(clusters, parts),
            in_specs=[
                pl.BlockSpec((1, CHUNK, order, order), fetched),
                pl.BlockSpec(memory_space=pltpu.VMEM),
            ],
            out_specs=pl.BlockSpec((1, CHUNK, order, order), lambda c, p, counts, rows: (c, p, 0, 0)),
        ),
        out_shape=jax.ShapeDtypeStruct(blocks.shape, BF16),
        compiler_params=pltpu.CompilerParams(vmem_limit_bytes=LIMIT),
        name="couplings",
    )(counts, rows, blocks, table)


def on_device(
    devices,
    columns,
    leaf_basis,
    transfer_leaf,
    transfer_mid,
    transfer_top,
    coupling_leaf,
    coupling_mid,
    partners_leaf,
    partners_mid,
    counts_leaf,
    counts_mid,
    ranks,
):
    leaf_count, points, order = leaf_basis.shape
    half = order // 2
    levels = leaf_count + 3
    vmem = pl.BlockSpec(memory_space=pltpu.VMEM)
    smem = pl.BlockSpec(memory_space=pltpu.SMEM)
    grams = pl.pallas_call(
        gram_kernel,
        out_shape=jax.ShapeDtypeStruct((levels, order, order), F32),
        in_specs=[vmem] * 4,
        out_specs=vmem,
        scratch_shapes=[
            pltpu.VMEM((2, order, order), F32),
            pltpu.VMEM((2, order, order), F32),
            pltpu.SemaphoreType.DMA((2,)),
            pltpu.SemaphoreType.DMA((2,)),
        ],
        compiler_params=pltpu.CompilerParams(
            collective_id=0, has_side_effects=True, vmem_limit_bytes=LIMIT
        ),
        name="grams",
    )(leaf_basis, transfer_leaf, transfer_mid, transfer_top)
    packed_rows = order + half + 16
    leaf_q, leaf_out, mid_out, top_full, packed, own = pl.pallas_call(
        tree_kernel,
        out_shape=(
            jax.ShapeDtypeStruct(leaf_basis.shape, BF16),
            jax.ShapeDtypeStruct(transfer_leaf.shape, F32),
            jax.ShapeDtypeStruct(transfer_mid.shape, F32),
            jax.ShapeDtypeStruct((order, order), F32),
            jax.ShapeDtypeStruct((packed_rows, order), F32),
            jax.ShapeDtypeStruct((3, order, order), BF16),
        ),
        in_specs=[smem] + [vmem] * 5,
        out_specs=[vmem] * 6,
        scratch_shapes=[pltpu.VMEM((levels, order, 2 * order), F32)],
        compiler_params=pltpu.CompilerParams(vmem_limit_bytes=LIMIT),
        name="tree",
    )(ranks, grams, leaf_basis, transfer_leaf, transfer_mid, transfer_top)
    sources = 2 * SPAN + 1
    table = pl.pallas_call(
        functools.partial(exchange_kernel, devices, columns),
        out_shape=jax.ShapeDtypeStruct((3 * sources, order, order), BF16),
        in_specs=[vmem] * 2,
        out_specs=vmem,
        scratch_shapes=[
            pltpu.VMEM((sources, packed_rows, order), F32),
            pltpu.SemaphoreType.DMA((sources,)),
            pltpu.SemaphoreType.DMA((sources,)),
        ],
        compiler_params=pltpu.CompilerParams(
            collective_id=1, has_side_effects=True, vmem_limit_bytes=LIMIT
        ),
        name="exchange",
    )(packed, own)
    col_index = lax.axis_index("col")
    base = SPAN - (lax.axis_index("row") * columns + col_index)
    leaf_rows = (partners_leaf // leaf_count + base) * 3 + partners_leaf % leaf_count
    mid_rows = (partners_mid + base) * 3 + 2
    top_out = lax.dynamic_slice_in_dim(top_full, col_index % 2 * half, half, 0)
    top_out = top_out.reshape(1, 1, half, order)
    coupling_leaf_out = transform(coupling_leaf, table, leaf_rows, counts_leaf, 0)
    coupling_mid_out = transform(coupling_mid, table, mid_rows, counts_mid, 2)
    return (leaf_q, leaf_out, mid_out, top_out, coupling_leaf_out, coupling_mid_out)


def solution(mesh):
    both = ("row", "col")
    in_specs = (
        P(both, None, None),
        P(both, None, None),
        P(both, None, None),
        P("row", None, None, None),
        P(both, None, None, None),
        P(both, None, None, None),
        P(both, None),
        P(both, None),
        P(both),
        P(both),
        P(),
    )
    out_specs = (
        P(both, None, None),
        P(both, None, None),
        P(both, None, None),
        P("row", "col", None, None),
        P(both, None, None, None),
        P(both, None, None, None),
    )
    columns = mesh.shape["col"]
    return jax.shard_map(
        functools.partial(on_device, mesh.shape["row"] * columns, columns),
        mesh=mesh,
        in_specs=in_specs,
        out_specs=out_specs,
        check_vma=False,
    )
```

profile of v0, /device:TPU:19, one launch (start us, length us, event | category | flops | bytes accessed | tf_op | source)
XLA Modules:
  0.0 105.1 jit_solution(10039654273055880785)
XLA Ops:
  1.3 0.7 multiply_add_fusion.rows
  2.0 0.7 fusion.rows
  2.6 0.0 copy-start
  2.7 1.2 %copy-done = bf16[2,2048,128]{2,1,0:T(8,128)(2,1)S(1)} copy-done((bf16[2,2048,128]{2,1,0:T(8,128)(2,1)S(1)}, bf16[2,2048,128]{2,1,0:T(8,128)(2,1)}, u32[]{:S(2)}) %copy-start) | copy-done | bytes 1048600
  3.9 0.0 copy-start.2
  3.9 0.9 copy-done.2
  4.8 0.0 copy-start.3
  4.8 0.9 copy-done.3
  5.7 0.0 copy-start.4
  5.7 0.8 copy-done.4
  6.5 0.0 copy-start.1
  6.5 6.4 %grams.1 = f32[5,128,128]{2,1,0:T(8,128)S(1)} custom-call(bf16[2,2048,128]{2,1,0:T(8,128)(2,1)S(1)} %copy-done, f32[2,128,128]{2,1,0:T(8,128)S(1)} %copy-done.2, f32[1,128,128]{2,1,0:T(8,128)S(1)} %copy-done.4, f32[1,2,128,128]{3,2,1,0:T(8,128)S(1)} %copy-done.3), custom_call_target="tpu_custom_call" | custom-call | tf_op jit(solution)/shard_map/grams/pallas_call | solution.py:325
  12.9 0.0 copy-start.6
  13.0 0.6 copy-done.6
  13.6 39.3 %tree.1 = (bf16[2,2048,128]{2,1,0:T(8,128)(2,1)}, f32[2,128,128]{2,1,0:T(8,128)}, f32[1,128,128]{2,1,0:T(8,128)}, f32[128,128]{1,0:T(8,128)S(1)}, f32[208,128]{1...) custom-call(s32[4]{0:T(128)S(1)} %copy-done.6, f32[5,128,128]{2,1,0:T(8,128)S(1)} %grams.1, bf16[2,2048,128]{2,1,0:T(8,128)(2,1)S(1)} %copy-done, ...), custom_call_target="tpu_custom_call" | custom-call | tf_op jit(solution)/shard_map/tree/pallas_call | solution.py:342
  52.9 0.6 dynamic-slice_bitcast_fusion
  53.6 24.8 %exchange.1.table = bf16[39,128,128]{2,1,0:T(8,128)(2,1)S(1)} custom-call(f32[208,128]{1,0:T(8,128)S(1)} %get-tuple-element.16.packed, bf16[3,128,128]{2,1,0:T(8,128)(2,1)S(1)} %get-tuple-element.17.own), custom_call_target="tpu_custom_call" | custom-call | tf_op jit(solution)/shard_map/exchange/pallas_call | solution.py:359
  78.3 0.0 copy-done.1
  78.4 0.0 copy-start.5
  78.4 9.6 %couplings.3 = bf16[1,112,128,128]{3,2,1,0:T(8,128)(2,1)} custom-call(s32[1]{0:T(128)S(6)} %copy.17.counts, s32[1,112]{1,0:T(1,128)S(1)} %multiply_add_fusion.rows, bf16[1,112,128,128]{3,2,1,0:T(8,128)(2,1)S(1)} %copy-done.1, bf16[39,128,128]{2,1,0:T(8,128)(2,1)S(1)} %exchange.1.table), custom_call_target="tpu_custom_call" | custom-call | tf_op jit(solution)/shard_map/couplings/pallas_call | solution.py:288
  88.0 0.0 copy-done.5
  88.0 17.1 %couplings.2 = bf16[2,112,128,128]{3,2,1,0:T(8,128)(2,1)} custom-call(s32[2]{0:T(128)S(1)} %copy-done.5, s32[2,112]{1,0:T(2,128)S(1)} %fusion.rows, bf16[2,112,128,128]{3,2,1,0:T(8,128)(2,1)} %blocks.2, bf16[39,128,128]{2,1,0:T(8,128)(2,1)S(1)} %exchange.1.table), custom_call_target="tpu_custom_call" | custom-call | tf_op jit(solution)/shard_map/couplings/pallas_call | solution.py:288
Async XLA Ops:
  2.6 1.2 %copy-start = (bf16[2,2048,128]{2,1,0:T(8,128)(2,1)S(1)}, bf16[2,2048,128]{2,1,0:T(8,128)(2,1)}, u32[]{:S(2)}) copy-start(bf16[2,2048,128]{2,1,0:T(8,128)(2,1)} %basis.3) | copy-start | bytes 3145732
  3.9 0.9 copy-start.2
  4.8 0.9 copy-start.3
  5.7 0.8 copy-start.4
  6.5 71.8 %copy-start.1 = (bf16[1,112,128,128]{3,2,1,0:T(8,128)(2,1)S(1)}, bf16[1,112,128,128]{3,2,1,0:T(8,128)(2,1)}, u32[]{:S(2)}) copy-start(bf16[1,112,128,128]{3,2,1,0:T(8,128)(2,1)} %blocks.3) | copy-start | bytes 11010052
  12.9 0.7 copy-start.6
  78.4 9.7 %copy-start.5 = (s32[2]{0:T(128)S(1)}, s32[2]{0:T(128)}, u32[]{:S(2)}) copy-start(s32[2]{0:T(128)} %counts.2) | copy-start | bytes 28
where the time goes:
time: 106 us; the launch traced here: 105 us
  Pallas kernels  97.3 us (92%)
  local copies, waits for them, and re-layouts  5.14 us (5%)
  other arithmetic  1.35 us (1%)
  between operations  1.35 us (1%)
    pallas_call x1, Pallas kernels, on_device(): pl.pallas_call(tree_kernel, out_shape=(jax.ShapeDtypeStruct(leaf_basis.sh...  39.3 us
    pallas_call x2, Pallas kernels, transform(): pl.pallas_call(functools.partial(coupling_kernel, own_first), grid_spec=p...  26.8 us
    pallas_call x1, Pallas kernels, on_device(): pl.pallas_call(functools.partial(exchange_kernel, devices, columns), out_...  24.8 us
    pallas_call x1, Pallas kernels, on_device(): pl.pallas_call(gram_kernel, out_shape=jax.ShapeDtypeStruct((levels, order...  6.41 us
    unnamed x14, local copies, waits for them, and re-layouts  4.53 us

commit v1 on v0

--- a/solution.py
+++ b/solution.py
@@ -85,38 +85,42 @@
 
     def panel(index, first_row):
         base = pl.multiple_of(index * PANEL, PANEL)
+        wides = [work[b, pl.ds(base, PANEL), :] for b in range(batch)]
+        columns = []
         for b in range(batch):
-            wide = work[b, pl.ds(base, PANEL), :]
-            turned = pltpu.roll(wide[:, :order], order - base, 1)
-            columns = [
-                jnp.broadcast_to(turned[:, r : r + 1], (PANEL, order)) for r in range(PANEL)
-            ]
-            for r in range(PANEL):
-                scale = lax.rsqrt(columns[r][r : r + 1, :])
-                coefficient = columns[r] * scale
+            turned = pltpu.roll(wides[b][:, :order], order - base, 1)
+            columns.append(
+                [jnp.broadcast_to(turned[:, r : r + 1], (PANEL, order)) for r in range(PANEL)]
+            )
+        for r in range(PANEL):
+            scales = [lax.rsqrt(columns[b][r][r : r + 1, :]) for b in range(batch)]
+            for b in range(batch):
+                scale = scales[b]
+                coefficient = jnp.where(narrow > r, columns[b][r] * scale, 0.0)
+                for q in range(r + 1, PANEL):
+                    columns[b][q] = columns[b][q] - coefficient * (
+                        columns[b][q][r : r + 1, :] * scale
+                    )
                 scale_wide = jnp.concatenate([scale, scale], axis=1)
                 coefficient_wide = jnp.concatenate([coefficient, coefficient], axis=1)
-                pivot_row = wide[r : r + 1, :] * scale_wide
-                wide = jnp.where(
-                    rows_in > r,
-                    wide - coefficient_wide * pivot_row,
-                    jnp.where(rows_in == r, pivot_row, wide),
+                pivot_row = wides[b][r : r + 1, :] * scale_wide
+                wides[b] = jnp.where(
+                    rows_in == r, pivot_row, wides[b] - coefficient_wide * pivot_row
                 )
-                for q in range(r + 1, PANEL):
-                    columns[q] = jnp.where(
-                        narrow > r,
-                        columns[q] - coefficient * (columns[q][r : r + 1, :] * scale),
-                        columns[q],
-                    )
-            wide = jnp.where((lanes >= order) | (lanes >= base + rows_in), wide, 0.0)
-            work[b, pl.ds(base, PANEL), :] = wide
+        keep = (lanes >= order) | (lanes >= base + rows_in)
+        wides = [jnp.where(keep, wide, 0.0) for wide in wides]
+        for b in range(batch):
+            work[b, pl.ds(base, PANEL), :] = wides[b]
+        changes = []
+        for wide in wides:
             after = jnp.where(lanes_narrow >= base + PANEL, wide[:, :order], 0.0)
             lh, lm, ll = three_parts(after)
             rh, rm, rl = three_parts(wide)
             left = jnp.concatenate([lh, lh, lm, lh, ll, lm], axis=0).astype(BF16)
             right = jnp.concatenate([rh, rm, rh, rl, rh, rm], axis=0).astype(BF16)
-            change = dot(left[:, first_row:], right, ((0,), (0,)))
-            work[b, first_row:, :] = work[b, first_row:, :] - change
+            changes.append(dot(left[:, first_row:], right, ((0,), (0,))))
+        for b in range(batch):
+            work[b, first_row:, :] = work[b, first_row:, :] - changes[b]
 
     panels = order // PANEL
     for group in range(GROUPS):
@@ -255,7 +259,7 @@
     count = counts[cluster]
     mine = table[3 * SPAN + own_first + cluster]
     start = part * CHUNK
-    step = 4
+    step = CHUNK
 
     for sub in range(0, CHUNK, step):
         slots = range(sub, sub + step)

time: 106 us -> 70.7 us (0.67)
  the two profiles are of different devices: /device:TPU:19 before, /device:TPU:13 now
where the time goes in v1:
time: 70.7 us; the launch traced here: 69.9 us
  Pallas kernels  62 us (88%)
  local copies, waits for them, and re-layouts  5.14 us (7%)
  other arithmetic  1.35 us (2%)
  between operations  1.35 us (2%)
    pallas_call x1, Pallas kernels, on_device(): pl.pallas_call(functools.partial(exchange_kernel, devices, columns), out_...  23.5 us
    pallas_call x2, Pallas kernels, transform(): pl.pallas_call(functools.partial(coupling_kernel, own_first), grid_spec=p...  19.8 us
    pallas_call x1, Pallas kernels, on_device(): pl.pallas_call(tree_kernel, out_shape=(jax.ShapeDtypeStruct(leaf_basis.sh...  11.7 us
    pallas_call x1, Pallas kernels, on_device(): pl.pallas_call(gram_kernel, out_shape=jax.ShapeDtypeStruct((levels, order...  7.06 us
    unnamed x14, local copies, waits for them, and re-layouts  4.53 us

profile of v1, /device:TPU:13, one launch (start us, length us, event | category | flops | bytes accessed | tf_op | source)
XLA Modules:
  0.0 69.9 jit_solution(8047884152858133378)
XLA Ops:
  1.3 0.7 multiply_add_fusion.rows
  2.0 0.7 fusion.rows
  2.6 0.0 copy-start
  2.7 1.2 %copy-done = bf16[2,2048,128]{2,1,0:T(8,128)(2,1)S(1)} copy-done((bf16[2,2048,128]{2,1,0:T(8,128)(2,1)S(1)}, bf16[2,2048,128]{2,1,0:T(8,128)(2,1)}, u32[]{:S(2)}) %copy-start) | copy-done | bytes 1048600
  3.9 0.0 copy-start.2
  3.9 0.9 %copy-done.2 = f32[2,128,128]{2,1,0:T(8,128)S(1)} copy-done((f32[2,128,128]{2,1,0:T(8,128)S(1)}, f32[2,128,128]{2,1,0:T(8,128)}, u32[]{:S(2)}) %copy-start.2) | copy-done | bytes 131096
  4.8 0.0 copy-start.3
  4.8 0.9 %copy-done.3 = f32[1,2,128,128]{3,2,1,0:T(8,128)S(1)} copy-done((f32[1,2,128,128]{3,2,1,0:T(8,128)S(1)}, f32[1,2,128,128]{3,2,1,0:T(8,128)}, u32[]{:S(2)}) %copy-start.3) | copy-done | bytes 131096
  5.7 0.0 copy-start.4
  5.7 0.8 %copy-done.4 = f32[1,128,128]{2,1,0:T(8,128)S(1)} copy-done((f32[1,128,128]{2,1,0:T(8,128)S(1)}, f32[1,128,128]{2,1,0:T(8,128)}, u32[]{:S(2)}) %copy-start.4) | copy-done | bytes 65560
  6.5 0.0 copy-start.1
  6.5 7.1 %grams.1 = f32[5,128,128]{2,1,0:T(8,128)S(1)} custom-call(bf16[2,2048,128]{2,1,0:T(8,128)(2,1)S(1)} %copy-done, f32[2,128,128]{2,1,0:T(8,128)S(1)} %copy-done.2, f32[1,128,128]{2,1,0:T(8,128)S(1)} %copy-done.4, f32[1,2,128,128]{3,2,1,0:T(8,128)S(1)} %copy-done.3), custom_call_target="tpu_custom_call" | custom-call | tf_op jit(solution)/shard_map/grams/pallas_call | solution.py:329
  13.6 0.0 copy-start.6
  13.6 0.6 copy-done.6
  14.3 11.7 %tree.1 = (bf16[2,2048,128]{2,1,0:T(8,128)(2,1)}, f32[2,128,128]{2,1,0:T(8,128)}, f32[1,128,128]{2,1,0:T(8,128)}, f32[128,128]{1,0:T(8,128)S(1)}, f32[208,128]{1...) custom-call(s32[4]{0:T(128)S(1)} %copy-done.6, f32[5,128,128]{2,1,0:T(8,128)S(1)} %grams.1, bf16[2,2048,128]{2,1,0:T(8,128)(2,1)S(1)} %copy-done, ...), custom_call_target="tpu_custom_call" | custom-call | tf_op jit(solution)/shard_map/tree/pallas_call | solution.py:346
  26.0 0.6 dynamic-slice_bitcast_fusion
  26.6 23.5 %exchange.1.table = bf16[39,128,128]{2,1,0:T(8,128)(2,1)S(1)} custom-call(f32[208,128]{1,0:T(8,128)S(1)} %get-tuple-element.16.packed, bf16[3,128,128]{2,1,0:T(8,128)(2,1)S(1)} %get-tuple-element.17.own), custom_call_target="tpu_custom_call" | custom-call | tf_op jit(solution)/shard_map/exchange/pallas_call | solution.py:363
  50.1 0.0 copy-done.1
  50.1 0.0 copy-start.5
  50.1 5.7 %couplings.3 = bf16[1,112,128,128]{3,2,1,0:T(8,128)(2,1)} custom-call(s32[1]{0:T(128)S(6)} %copy.17.counts, s32[1,112]{1,0:T(1,128)S(1)} %multiply_add_fusion.rows, bf16[1,112,128,128]{3,2,1,0:T(8,128)(2,1)S(1)} %copy-done.1, bf16[39,128,128]{2,1,0:T(8,128)(2,1)S(1)} %exchange.1.table), custom_call_target="tpu_custom_call" | custom-call | tf_op jit(solution)/shard_map/couplings/pallas_call | solution.py:292
  55.8 0.0 copy-done.5
  55.8 14.1 %couplings.2 = bf16[2,112,128,128]{3,2,1,0:T(8,128)(2,1)} custom-call(s32[2]{0:T(128)S(1)} %copy-done.5, s32[2,112]{1,0:T(2,128)S(1)} %fusion.rows, bf16[2,112,128,128]{3,2,1,0:T(8,128)(2,1)} %blocks.2, bf16[39,128,128]{2,1,0:T(8,128)(2,1)S(1)} %exchange.1.table), custom_call_target="tpu_custom_call" | custom-call | tf_op jit(solution)/shard_map/couplings/pallas_call | solution.py:292
Async XLA Ops:
  2.6 1.2 %copy-start = (bf16[2,2048,128]{2,1,0:T(8,128)(2,1)S(1)}, bf16[2,2048,128]{2,1,0:T(8,128)(2,1)}, u32[]{:S(2)}) copy-start(bf16[2,2048,128]{2,1,0:T(8,128)(2,1)} %basis.3) | copy-start | bytes 3145732
  3.9 0.9 %copy-start.2 = (f32[2,128,128]{2,1,0:T(8,128)S(1)}, f32[2,128,128]{2,1,0:T(8,128)}, u32[]{:S(2)}) copy-start(f32[2,128,128]{2,1,0:T(8,128)} %t_leaf.3) | copy-start | bytes 393220
  4.8 0.9 %copy-start.3 = (f32[1,2,128,128]{3,2,1,0:T(8,128)S(1)}, f32[1,2,128,128]{3,2,1,0:T(8,128)}, u32[]{:S(2)}) copy-start(f32[1,2,128,128]{3,2,1,0:T(8,128)} %t_top.3) | copy-start | bytes 393220
  5.7 0.8 %copy-start.4 = (f32[1,128,128]{2,1,0:T(8,128)S(1)}, f32[1,128,128]{2,1,0:T(8,128)}, u32[]{:S(2)}) copy-start(f32[1,128,128]{2,1,0:T(8,128)} %t_mid.3) | copy-start | bytes 196612
  6.5 43.6 %copy-start.1 = (bf16[1,112,128,128]{3,2,1,0:T(8,128)(2,1)S(1)}, bf16[1,112,128,128]{3,2,1,0:T(8,128)(2,1)}, u32[]{:S(2)}) copy-start(bf16[1,112,128,128]{3,2,1,0:T(8,128)(2,1)} %blocks.3) | copy-start | bytes 11010052
  13.6 0.7 copy-start.6
  50.1 5.7 %copy-start.5 = (s32[2]{0:T(128)S(1)}, s32[2]{0:T(128)}, u32[]{:S(2)}) copy-start(s32[2]{0:T(128)} %counts.2) | copy-start | bytes 28

commit v2 on v1

--- a/solution.py
+++ b/solution.py
@@ -134,7 +134,7 @@
         lax.fori_loop(first, last, body, 0)
 
 
-def tree_kernel(ranks, grams, basis, t_leaf, t_mid, t_top, leaf_q, leaf_out, mid_out, top_out, packed, own, work):
+def tree_kernel(ranks, grams, basis, t_leaf, t_mid, t_top, leaf_q, leaf_out, mid_out, top_out, packed, own, work, top_full):
     leaf_count = basis.shape[0]
     order = grams.shape[1]
     half = order // 2
@@ -163,7 +163,9 @@
         leaf_q[leaf] = dot(basis[leaf], weights, ((1,), (1,))).astype(BF16)
         leaf_out[leaf] = moved(leaf, 0, t_leaf[leaf], mid, 1)
     mid_out[0] = moved(mid, 1, t_mid[0], above, 2)
-    top_out[...] = moved(above, 2, t_top[0, pair], quad, 3)
+    top_full[...] = moved(above, 2, t_top[0, pair], quad, 3)
+    side = lax.rem(lax.axis_index("col"), 2)
+    top_out[...] = top_full[pl.ds(pl.multiple_of(side * half, half), half), :]
     first, second, third = factor(0, 0), factor(1, 0), factor(mid, 1)
     own[0] = first.astype(BF16)
     own[1] = second.astype(BF16)
@@ -185,79 +187,118 @@
 def exchange_kernel(devices, columns, packed, own, table, landed, send_sem, recv_sem):
     order = own.shape[1]
     half = order // 2
+    leaf_count = own.shape[0] - 1
     here = lax.axis_index("row") * columns + lax.axis_index("col")
+    reach = (SPAN + 1) // 2
+    sources = 2 * (2 * reach + 1)
+    groups = devices // 2
+    group = lax.div(here, 2)
+    parity = here - 2 * group
+    sibling = here + 1 - 2 * parity
     barrier = pltpu.get_barrier_semaphore()
-    offsets = [sign * away for away in range(1, SPAN + 1) for sign in (1, -1)]
+    offsets = [sign * away for away in range(1, reach + 1) for sign in (1, -1)]
 
     def place(index):
         return (lax.div(index, columns), lax.rem(index, columns))
 
-    def inside(index):
-        return (index >= 0) & (index < devices)
+    def inside(offset):
+        return (group + offset >= 0) & (group + offset < groups)
 
     for offset in offsets:
-        @pl.when(inside(here + offset))
-        def _():
-            pl.semaphore_signal(barrier, inc=1, device_id=place(here + offset), device_id_type=MESH)
-    peers = jnp.minimum(here, SPAN) + jnp.minimum(devices - 1 - here, SPAN)
+        @pl.when(inside(offset))
+        def _():
+            pl.semaphore_signal(
+                barrier, inc=1, device_id=place(here + 2 * offset), device_id_type=MESH
+            )
+    pl.semaphore_signal(barrier, inc=1, device_id=place(sibling), device_id_type=MESH)
+    peers = jnp.minimum(group, reach) + jnp.minimum(groups - 1 - group, reach) + 1
     pl.semaphore_wait(barrier, peers)
 
-    def copy_to(offset):
-        slot = SPAN - offset
+    def copy(source, slot, sem, target):
         return pltpu.make_async_remote_copy(
-            src_ref=packed,
+            src_ref=source,
             dst_ref=landed.at[slot],
-            send_sem=send_sem.at[slot],
+            send_sem=send_sem.at[sem],
             recv_sem=recv_sem.at[slot],
-            device_id=place(here + offset),
+            device_id=place(target),
             device_id_type=MESH,
         )
 
-    for offset in reversed(offsets):
-        @pl.when(inside(here + offset))
-        def _():
-            copy_to(offset).start()
-    for k in range(3):
-        table[3 * SPAN + k] = own[k]
+    def direct(offset):
+        return copy(packed, 2 * (reach - offset) + parity, reach - offset, here + 2 * offset)
+
+    def onward(offset, side):
+        slot = 2 * (reach + offset) + side
+        return copy(landed.at[slot], slot, 3 * reach + 1 + offset, sibling)
+
+    beside = copy(packed, 2 * reach + parity, reach, sibling)
+    order_sent = offsets[::-1]
+    for offset in order_sent:
+        @pl.when(inside(offset))
+        def _():
+            direct(offset).start()
+    beside.start()
+    for k in range(leaf_count):
+        table[leaf_count * (2 * reach + parity) + k] = own[k]
+    table[leaf_count * sources + 2 * reach + parity] = own[leaf_count]
     row_id = lax.broadcasted_iota(jnp.int32, (order, order), 0)
     col_id = lax.broadcasted_iota(jnp.int32, (order, order), 1)
+
+    def unpack(slot):
+        both = landed[slot, :order, :]
+        upper = jnp.where(col_id >= row_id, both, 0.0)
+        lower = jnp.where(
+            col_id == row_id,
+            landed[slot, order + half : order + half + 1, :],
+            jnp.where(col_id < row_id, both, 0.0),
+        )
+        table[leaf_count * slot] = upper.astype(BF16)
+        table[leaf_count * slot + 1] = lower.T.astype(BF16)
+        folded = landed[slot, order : order + half, :]
+        rows = row_id[:half]
+        lanes = col_id[:half]
+        middle = leaf_count * sources + slot
+        table[middle, :half, :] = jnp.where(lanes >= rows, folded, 0.0).astype(BF16)
+        corner = jnp.where(lanes < rows, folded, 0.0)
+        corner = jnp.concatenate([corner, jnp.zeros_like(corner)], axis=0).T
+        corner = pltpu.roll(corner[:half], half, 1)
+        corner = jnp.where(
+            lanes == rows + half, landed[slot, order + half + 8 : order + half + 9, :], corner
+        )
+        table[middle, half:, :] = corner.astype(BF16)
+
+    other = 1 - parity
+    copy(packed, 2 * reach + other, reach, sibling).wait_recv()
+    unpack(2 * reach + other)
     for offset in offsets:
-        slot = SPAN + offset
-
-        @pl.when(inside(here + offset))
-        def _():
-            copy_to(-offset).wait_recv()
-            both = landed[slot, :order, :]
-            upper = jnp.where(col_id >= row_id, both, 0.0)
-            lower = jnp.where(
-                col_id == row_id,
-                landed[slot, order + half : order + half + 1, :],
-                jnp.where(col_id < row_id, both, 0.0),
-            )
-            table[3 * slot] = upper.astype(BF16)
-            table[3 * slot + 1] = lower.T.astype(BF16)
-            folded = landed[slot, order : order + half, :]
-            rows = row_id[:half]
-            lanes = col_id[:half]
-            table[3 * slot + 2, :half, :] = jnp.where(lanes >= rows, folded, 0.0).astype(BF16)
-            corner = jnp.where(lanes < rows, folded, 0.0)
-            corner = jnp.concatenate([corner, jnp.zeros_like(corner)], axis=0).T
-            corner = pltpu.roll(corner[:half], half, 1)
-            corner = jnp.where(
-                lanes == rows + half, landed[slot, order + half + 8 : order + half + 9, :], corner
-            )
-            table[3 * slot + 2, half:, :] = corner.astype(BF16)
-
+        @pl.when(inside(offset))
+        def _():
+            direct(-offset).wait_recv()
+            onward(offset, parity).start()
+            unpack(2 * (reach + offset) + parity)
     for offset in offsets:
-        @pl.when(inside(here + offset))
-        def _():
-            copy_to(offset).wait_send()
-
-
-def coupling_kernel(own_first, counts, rows, blocks, table, out):
+        @pl.when(inside(offset))
+        def _():
+            onward(offset, other).wait_recv()
+            unpack(2 * (reach + offset) + other)
+    for offset in offsets:
+        @pl.when(inside(offset))
+        def _():
+            direct(offset).wait_send()
+            onward(offset, parity).wait_send()
+    beside.wait_send()
+
+
+def coupling_kernel(own_first, leaf_count, columns, counts, partners, blocks, own, table, out):
     cluster, part = pl.program_id(0), pl.program_id(1)
     count = counts[cluster]
-    mine = table[3 * SPAN + own_first + cluster]
+    mine = own[own_first + cluster]
+    here = lax.axis_index("row") * columns + lax.axis_index("col")
+    reach = (SPAN + 1) // 2
+    base = 2 * reach - (here - lax.rem(here, 2))
+    shift = leaf_count * base
+    if own_first:
+        shift = leaf_count * 2 * (2 * reach + 1) + base
     start = part * CHUNK
     step = CHUNK
 
@@ -274,7 +315,7 @@
             order = mine.shape[0]
             for s in slots:
                 left = lefts[(s - sub) // 2][:, (s - sub) % 2 * order : ((s - sub) % 2 + 1) * order]
-                result = dot(left, table[rows[cluster, start + s]], ((1,), (1,)))
+                result = dot(left, table[partners[cluster, start + s] + shift], ((1,), (1,)))
                 out[0, s] = jnp.where(start + s < count, result, 0.0).astype(BF16)
 
         @pl.when(start + sub >= count)
@@ -282,28 +323,29 @@
             out[0, sub : sub + step] = jnp.zeros((step,) + out.shape[2:], BF16)
 
 
-def transform(blocks, table, rows, counts, own_first):
+def transform(blocks, own, table, partners, counts, own_first, columns):
     clusters, slots, order, _ = blocks.shape
     parts = slots // CHUNK
 
-    def fetched(c, p, counts, rows):
+    def fetched(c, p, counts, partners):
         return (c, jnp.minimum(p, lax.div(counts[c] - 1, CHUNK)), 0, 0)
 
     return pl.pallas_call(
-        functools.partial(coupling_kernel, own_first),
+        functools.partial(coupling_kernel, own_first, own.shape[0] - 1, columns),
         grid_spec=pltpu.PrefetchScalarGridSpec(
             num_scalar_prefetch=2,
             grid=(clusters, parts),
             in_specs=[
                 pl.BlockSpec((1, CHUNK, order, order), fetched),
                 pl.BlockSpec(memory_space=pltpu.VMEM),
+                pl.BlockSpec(memory_space=pltpu.VMEM),
             ],
-            out_specs=pl.BlockSpec((1, CHUNK, order, order), lambda c, p, counts, rows: (c, p, 0, 0)),
+            out_specs=pl.BlockSpec((1, CHUNK, order, order), lambda c, p, counts, partners: (c, p, 0, 0)),
         ),
         out_shape=jax.ShapeDtypeStruct(blocks.shape, BF16),
         compiler_params=pltpu.CompilerParams(vmem_limit_bytes=LIMIT),
         name="couplings",
-    )(counts, rows, blocks, table)
+    )(counts, partners, blocks, own, table)
 
 
 def on_device(
@@ -343,23 +385,26 @@
         name="grams",
     )(leaf_basis, transfer_leaf, transfer_mid, transfer_top)
     packed_rows = order + half + 16
-    leaf_q, leaf_out, mid_out, top_full, packed, own = pl.pallas_call(
+    leaf_q, leaf_out, mid_out, top_half, packed, own = pl.pallas_call(
         tree_kernel,
         out_shape=(
             jax.ShapeDtypeStruct(leaf_basis.shape, BF16),
             jax.ShapeDtypeStruct(transfer_leaf.shape, F32),
             jax.ShapeDtypeStruct(transfer_mid.shape, F32),
-            jax.ShapeDtypeStruct((order, order), F32),
+            jax.ShapeDtypeStruct((half, order), F32),
             jax.ShapeDtypeStruct((packed_rows, order), F32),
             jax.ShapeDtypeStruct((3, order, order), BF16),
         ),
         in_specs=[smem] + [vmem] * 5,
         out_specs=[vmem] * 6,
-        scratch_shapes=[pltpu.VMEM((levels, order, 2 * order), F32)],
+        scratch_shapes=[
+            pltpu.VMEM((levels, order, 2 * order), F32),
+            pltpu.VMEM((order, order), F32),
+        ],
         compiler_params=pltpu.CompilerParams(vmem_limit_bytes=LIMIT),
         name="tree",
     )(ranks, grams, leaf_basis, transfer_leaf, transfer_mid, transfer_top)
-    sources = 2 * SPAN + 1
+    sources = 2 * (2 * ((SPAN + 1) // 2) + 1)
     table = pl.pallas_call(
         functools.partial(exchange_kernel, devices, columns),
         out_shape=jax.ShapeDtypeStruct((3 * sources, order, order), BF16),
@@ -375,14 +420,13 @@
         ),
         name="exchange",
     )(packed, own)
-    col_index = lax.axis_index("col")
-    base = SPAN - (lax.axis_index("row") * columns + col_index)
-    leaf_rows = (partners_leaf // leaf_count + base) * 3 + partners_leaf % leaf_count
-    mid_rows = (partners_mid + base) * 3 + 2
-    top_out = lax.dynamic_slice_in_dim(top_full, col_index % 2 * half, half, 0)
-    top_out = top_out.reshape(1, 1, half, order)
-    coupling_leaf_out = transform(coupling_leaf, table, leaf_rows, counts_leaf, 0)
-    coupling_mid_out = transform(coupling_mid, table, mid_rows, counts_mid, 2)
+    top_out = top_half.reshape(1, 1, half, order)
+    coupling_leaf_out = transform(
+        coupling_leaf, own, table, partners_leaf, counts_leaf, 0, columns
+    )
+    coupling_mid_out = transform(
+        coupling_mid, own, table, partners_mid, counts_mid, leaf_count, columns
+    )
     return (leaf_q, leaf_out, mid_out, top_out, coupling_leaf_out, coupling_mid_out)
 
 

time: 70.7 us -> 60.8 us (0.86)
  the two profiles are of different devices: /device:TPU:13 before, /device:TPU:23 now
where the time goes in v2:
time: 60.8 us; the launch traced here: 60.9 us
  Pallas kernels  55 us (90%)
  local copies, waits for them, and re-layouts  4.54 us (7%)
  between operations  1.37 us (2%)
    pallas_call x2, Pallas kernels, transform(): pl.pallas_call(functools.partial(coupling_kernel, own_first, own.shape[0]...  21.5 us
    pallas_call x1, Pallas kernels, on_device(): pl.pallas_call(functools.partial(exchange_kernel, devices, columns), out_...  15.3 us
    pallas_call x1, Pallas kernels, on_device(): pl.pallas_call(tree_kernel, out_shape=(jax.ShapeDtypeStruct(leaf_basis.sh...  11.7 us
    pallas_call x1, Pallas kernels, on_device(): pl.pallas_call(gram_kernel, out_shape=jax.ShapeDtypeStruct((levels, order...  6.41 us
    unnamed x18, local copies, waits for them, and re-layouts  4.54 us

profile of v2, /device:TPU:23, one launch (start us, length us, event | category | flops | bytes accessed | tf_op | source)
XLA Modules:
  0.0 60.9 jit_solution(16703132816191791586)
XLA Ops:
  0.6 0.0 copy-start.8
  1.3 0.0 copy-start
  1.3 1.2 %copy-done = bf16[2,2048,128]{2,1,0:T(8,128)(2,1)S(1)} copy-done((bf16[2,2048,128]{2,1,0:T(8,128)(2,1)S(1)}, bf16[2,2048,128]{2,1,0:T(8,128)(2,1)}, u32[]{:S(2)}) %copy-start) | copy-done | bytes 1048600
  2.5 0.0 copy-start.2
  2.5 0.9 %copy-done.2 = f32[2,128,128]{2,1,0:T(8,128)S(1)} copy-done((f32[2,128,128]{2,1,0:T(8,128)S(1)}, f32[2,128,128]{2,1,0:T(8,128)}, u32[]{:S(2)}) %copy-start.2) | copy-done | bytes 131096
  3.4 0.0 copy-start.3
  3.4 0.9 %copy-done.3 = f32[1,2,128,128]{3,2,1,0:T(8,128)S(1)} copy-done((f32[1,2,128,128]{3,2,1,0:T(8,128)S(1)}, f32[1,2,128,128]{3,2,1,0:T(8,128)}, u32[]{:S(2)}) %copy-start.3) | copy-done | bytes 131096
  4.3 0.0 copy-start.4
  4.3 0.8 %copy-done.4 = f32[1,128,128]{2,1,0:T(8,128)S(1)} copy-done((f32[1,128,128]{2,1,0:T(8,128)S(1)}, f32[1,128,128]{2,1,0:T(8,128)}, u32[]{:S(2)}) %copy-start.4) | copy-done | bytes 65560
  5.2 0.0 copy-start.1
  5.2 6.4 %grams.1 = f32[5,128,128]{2,1,0:T(8,128)S(1)} custom-call(bf16[2,2048,128]{2,1,0:T(8,128)(2,1)S(1)} %copy-done, f32[2,128,128]{2,1,0:T(8,128)S(1)} %copy-done.2, f32[1,128,128]{2,1,0:T(8,128)S(1)} %copy-done.4, f32[1,2,128,128]{3,2,1,0:T(8,128)S(1)} %copy-done.3), custom_call_target="tpu_custom_call" | custom-call | tf_op jit(solution)/shard_map/grams/pallas_call | solution.py:371
  11.6 0.0 copy-start.7
  11.6 0.6 %copy-done.7 = s32[4]{0:T(128)S(1)} copy-done((s32[4]{0:T(128)S(1)}, s32[4]{0:T(128)}, u32[]{:S(2)}) %copy-start.7) | copy-done | bytes 40
  12.3 11.7 %tree.1 = (bf16[2,2048,128]{2,1,0:T(8,128)(2,1)}, f32[2,128,128]{2,1,0:T(8,128)}, f32[1,128,128]{2,1,0:T(8,128)}, f32[64,128]{1,0:T(8,128)}, f32[208,128]{1,0:T(8,128)S(1)}, /*index=5*/bf16[3,128,128]{2,1,0:T(8,128)(2,1)S(1)}) custom-call(s32[4]{0:T(128)S(1)} %copy-done.7, f32[5,128,128]{2,1,0:T(8,128)S(1)} %grams.1, bf16[2,2048,128]{2,1,0:T(8,128)(2,1)S(1)} %copy-done, ...), custom_call_target="tpu_custom_call" | custom-call | tf_op jit(solution)/shard_map/tree/pallas_call | solution.py:388
  24.0 15.3 %exchange.1.table = bf16[42,128,128]{2,1,0:T(8,128)(2,1)S(1)} custom-call(f32[208,128]{1,0:T(8,128)S(1)} %get-tuple-element.17.packed, bf16[3,128,128]{2,1,0:T(8,128)(2,1)S(1)} %get-tuple-element.16.own), custom_call_target="tpu_custom_call" | custom-call | tf_op jit(solution)/shard_map/exchange/pallas_call | solution.py:408
  39.3 0.0 copy-done.8
  39.4 0.0 copy-done.1
  39.4 0.0 copy-start.5
  39.4 0.0 copy-start.6
  39.4 6.3 %couplings.3 = bf16[1,112,128,128]{3,2,1,0:T(8,128)(2,1)} custom-call(s32[1]{0:T(128)S(6)} %copy.17.counts, s32[1,112]{1,0:T(1,128)S(1)} %copy-done.8, bf16[1,112,128,128]{3,2,1,0:T(8,128)(2,1)S(1)} %copy-done.1, bf16[3,128,128]{2,1,0:T(8,128)(2,1)S(1)} %get-tuple-element.16.own, bf16[42,128,128]{2,1,0:T(8,128)(2,1)S(1)} %exchange.1.table), custom_call_target="tpu_custom_call" | custom-call | tf_op jit(solution)/shard_map/couplings/pallas_call | solution.py:333
  45.6 0.0 copy-done.5
  45.7 0.0 copy-done.6
  45.7 15.3 %couplings.2 = bf16[2,112,128,128]{3,2,1,0:T(8,128)(2,1)} custom-call(s32[2]{0:T(128)S(1)} %copy-done.6, s32[2,112]{1,0:T(2,128)S(1)} %copy-done.5, bf16[2,112,128,128]{3,2,1,0:T(8,128)(2,1)} %blocks.2, bf16[3,128,128]{2,1,0:T(8,128)(2,1)S(1)} %get-tuple-element.16.own, bf16[42,128,128]{2,1,0:T(8,128)(2,1)S(1)} %exchange.1.table), custom_call_target="tpu_custom_call" | custom-call | tf_op jit(solution)/shard_map/couplings/pallas_call | solution.py:333
Async XLA Ops:
  0.6 38.7 %copy-start.8 = (s32[1,112]{1,0:T(1,128)S(1)}, s32[1,112]{1,0:T(1,128)}, u32[]{:S(2)}) copy-start(s32[1,112]{1,0:T(1,128)} %partners.3) | copy-start | bytes 1348
  1.3 1.2 %copy-start = (bf16[2,2048,128]{2,1,0:T(8,128)(2,1)S(1)}, bf16[2,2048,128]{2,1,0:T(8,128)(2,1)}, u32[]{:S(2)}) copy-start(bf16[2,2048,128]{2,1,0:T(8,128)(2,1)} %basis.3) | copy-start | bytes 3145732
  2.5 0.9 %copy-start.2 = (f32[2,128,128]{2,1,0:T(8,128)S(1)}, f32[2,128,128]{2,1,0:T(8,128)}, u32[]{:S(2)}) copy-start(f32[2,128,128]{2,1,0:T(8,128)} %t_leaf.3) | copy-start | bytes 393220
  3.4 0.9 %copy-start.3 = (f32[1,2,128,128]{3,2,1,0:T(8,128)S(1)}, f32[1,2,128,128]{3,2,1,0:T(8,128)}, u32[]{:S(2)}) copy-start(f32[1,2,128,128]{3,2,1,0:T(8,128)} %t_top.3) | copy-start | bytes 393220
  4.3 0.8 %copy-start.4 = (f32[1,128,128]{2,1,0:T(8,128)S(1)}, f32[1,128,128]{2,1,0:T(8,128)}, u32[]{:S(2)}) copy-start(f32[1,128,128]{2,1,0:T(8,128)} %t_mid.3) | copy-start | bytes 196612
  5.2 34.2 %copy-start.1 = (bf16[1,112,128,128]{3,2,1,0:T(8,128)(2,1)S(1)}, bf16[1,112,128,128]{3,2,1,0:T(8,128)(2,1)}, u32[]{:S(2)}) copy-start(bf16[1,112,128,128]{3,2,1,0:T(8,128)(2,1)} %blocks.3) | copy-start | bytes 11010052
  11.6 0.7 %copy-start.7 = (s32[4]{0:T(128)S(1)}, s32[4]{0:T(128)}, u32[]{:S(2)}) copy-start(s32[4]{0:T(128)} %ranks.1) | copy-start | bytes 52
  39.4 6.3 %copy-start.5 = (s32[2,112]{1,0:T(2,128)S(1)}, s32[2,112]{1,0:T(2,128)}, u32[]{:S(2)}) copy-start(s32[2,112]{1,0:T(2,128)} %partners.2) | copy-start | bytes 2692
  39.4 6.3 %copy-start.6 = (s32[2]{0:T(128)S(1)}, s32[2]{0:T(128)}, u32[]{:S(2)}) copy-start(s32[2]{0:T(128)} %counts.2) | copy-start | bytes 28
